TPU v7x, 128 devices: a whole 4x4x4 slice. The times are simulated.
128 devices in a mesh: tm: 8 (over z, core), map: 16 (over x, y).
Axes of the slice: x: 4, y: 4, z: 4, core: 2. Of those that a mesh axis runs over, the one named last changes fastest.
Arguments:
- points: float32 [3, 524288, 128], P(None, ('tm', 'map')), may hold values from -6 to 6
- poses: float32 [6, 4096], P(None, ('tm', 'map')), may hold values from -1.5 to 1.5
- normal_angles: float32 [2, 32768], P(None, ('tm', 'map')), may hold values from -3.140625 to 3.140625
- voxel_ids: int32 [524288], P(('tm', 'map')), may hold values from -1 to 32767, as said below
- scan_ids: int32 [524288], P(('tm', 'map')), may hold values from 0 to 511
Outputs:
- hessian: float32 [36, 4096], P(None, ('tm', 'map'))
- gradient: float32 [6, 4096], P(None, ('tm', 'map'))
- plane_cost: float32 [32768], P(('tm', 'map'))
Inputs may be any that keep to these rules, and one draw needn't show every extreme that they name: `voxel_ids`: -1 marks an empty slot. Otherwise the block at position s among the 4096 blocks of its device has its voxel among those of owner o = s // 32, that is, in [o * 256, (o + 1) * 256), where owners are devices in tm+map order. In every draw some owner gets a live block in every slot from every device.
All inputs are finite; a program needn't handle non-finite values.
Results may differ from a plain program's by a relative error of at most 0.0003.
Values sent between devices are 32-bit elements; how exact they have to be, the bound alone decides.
No kernel may reach another device: no remote copies, remote signals or barrier semaphores. Data moves between devices by JAX's collectives and lax.ppermute only.
A program may use at most 128 MiB of HBM per device.

v0:
```python
import functools

import jax
import jax.numpy as jnp
from jax import lax
from jax.experimental import pallas as pl
from jax.experimental.pallas import tpu as pltpu
from jax.sharding import PartitionSpec as P

LANES = 128
GROUPS = 4
SLOTS = 32
PTS = 128
SENT_ROWS = 5
ROWS = 32
TM = 8
SCAN_ROW = 512
VOX = 256
BF16 = jnp.bfloat16
F32 = jnp.float32


def swap_groups(rows):
    lane = lax.broadcasted_iota(jnp.int32, rows[0].shape, 1) // SLOTS
    out = []
    for g in range(GROUPS):
        acc = None
        for h in range(GROUPS):
            shift = (h - g) * SLOTS % LANES
            part = rows[h] if shift == 0 else pltpu.roll(rows[h], shift, 1)
            acc = part if acc is None else jnp.where(lane == h, part, acc)
        out.append(acc)
    return out


def split3(x):
    hi = x.astype(BF16)
    rest = x - hi.astype(F32)
    mid = rest.astype(BF16)
    lo = (rest - mid.astype(F32)).astype(BF16)
    return jnp.concatenate([hi, mid, lo], axis=0)


def fold3(x):
    n = x.shape[0] // 3
    return x[:n] + x[n : 2 * n] + x[2 * n :]


def moments_kernel(points_ref, vox_ref, scan_ref, poses_ref, sent_ref, acc_ref):
    step = pl.program_id(0)
    chunks = points_ref.shape[1] // LANES
    for cc in range(chunks):
        span = pl.ds(cc * LANES, LANES)
        x = points_ref[0, span, :].T
        y = points_ref[1, span, :].T
        z = points_ref[2, span, :].T
        quantities = [x, y, z, x * x, y * y, z * z, x * y, x * z, y * z]
        for f, q in enumerate(quantities):
            acc_ref[f, pl.ds(step * chunks + cc, 1), :] = jnp.sum(q, axis=0, keepdims=True)

    @pl.when(step == pl.num_programs(0) - 1)
    def _():
        lane = lax.broadcasted_iota(jnp.int32, (ROWS, LANES), 1)
        row = lax.broadcasted_iota(jnp.int32, (ROWS, LANES), 0)
        vox = vox_ref[...]
        owner = row * GROUPS + lane // SLOTS
        vox = jnp.where(vox >= 0, vox - owner * VOX, -1).astype(F32)
        scan = scan_ref[...].astype(F32)
        p = poses_ref[...]
        p = jnp.concatenate([p, p, p, p], axis=1)
        cos, sin = jnp.cos(p[:3]), jnp.sin(p[:3])
        one = [cos[0:1], sin[0:1], cos[1:2], sin[1:2], cos[2:3], sin[2:3], p[3:4], p[4:5], p[5:6]]
        group = lax.broadcasted_iota(jnp.int32, (1, LANES), 1) // SLOTS
        f = [acc_ref[i] for i in range(9)]
        whole = lambda r: jnp.broadcast_to(r, (ROWS, LANES))
        k0 = swap_groups(f[0:4])
        k1 = swap_groups(f[4:8])
        k2 = swap_groups([f[8], vox, scan, whole(one[0])])

        def four(rs):
            r = jnp.where(group == 0, rs[0], jnp.where(group == 1, rs[1], jnp.where(group == 2, rs[2], rs[3])))
            return whole(r)

        k3 = four(one[1:5])
        k4 = four(one[5:9])
        for g in range(GROUPS):
            for k, v in enumerate([k0[g], k1[g], k2[g], k3, k4]):
                sent_ref[pl.ds(g * SENT_ROWS + k, ROWS, stride=GROUPS * SENT_ROWS), :] = v


def owner_kernel(recv_ref, angles_ref, out_ref, cost_ref, tab_ref, gat_ref, hot_ref, vhot_ref, feat_ref):
    feats = []
    for k in range(SENT_ROWS):
        rows = [recv_ref[pl.ds(h * SENT_ROWS + k, ROWS, stride=GROUPS * SENT_ROWS), :] for h in range(GROUPS)]
        feats += swap_groups(rows)
    p1 = feats[0:3]
    pxx, pyy, pzz, pxy, pxz, pyz = feats[3:9]
    vox = feats[9].astype(jnp.int32)
    scan = feats[10].astype(jnp.int32)
    cx, sx, cy, sy, cz, sz, tx, ty, tz = feats[11:20]
    table = [
        cz * cy,
        cz * sy * sx - sz * cx,
        cz * sy * cx + sz * sx,
        sz * cy,
        sz * sy * sx + cz * cx,
        sz * sy * cx - cz * sx,
        -sy,
        cy * sx,
        cy * cx,
        tx,
        ty,
        tz,
    ]
    zeros = jnp.zeros((ROWS, LANES), F32)
    for f in range(16):
        tab_ref[pl.ds(f, ROWS, stride=16), :] = table[f] if f < 12 else zeros

    def wide(ref, t, n):
        return jnp.concatenate([ref[pl.ds((t * 4 + i) * n, n), :] for i in range(4)], axis=1)

    def put(ref, t, n, val):
        for i in range(4):
            ref[pl.ds((t * 4 + i) * n, n), :] = val[:, i * LANES : (i + 1) * LANES]

    scan_iota = lax.broadcasted_iota(jnp.int32, (SCAN_ROW, LANES), 0)
    vox_iota = lax.broadcasted_iota(jnp.int32, (VOX, LANES), 0)
    for t in range(TM):
        for i in range(4):
            r = 4 * t + i
            hot_ref[t, :, i * LANES : (i + 1) * LANES] = jnp.where(scan_iota == scan[r : r + 1, :], 1.0, 0.0).astype(BF16)
            vhot_ref[:, r * LANES : (r + 1) * LANES] = jnp.where(vox_iota == vox[r : r + 1, :], 1.0, 0.0).astype(BF16)
        got = jnp.dot(split3(wide(tab_ref, t, 16)), hot_ref[t], preferred_element_type=F32)
        put(gat_ref, t, 16, fold3(got))

    rot = [[gat_ref[pl.ds(3 * i + j, ROWS, stride=16), :] for j in range(3)] for i in range(3)]
    tr = [gat_ref[pl.ds(9 + i, ROWS, stride=16), :] for i in range(3)]
    second = [[pxx, pxy, pxz], [pxy, pyy, pyz], [pxz, pyz, pzz]]
    rp = [sum(rot[i][j] * p1[j] for j in range(3)) for i in range(3)]
    half = [[sum(rot[i][k] * second[k][j] for k in range(3)) for j in range(3)] for i in range(3)]
    m1 = [rp[i] + PTS * tr[i] for i in range(3)]
    m2 = {}
    for i, j in [(0, 0), (1, 1), (2, 2), (0, 1), (0, 2), (1, 2)]:
        m2[i, j] = sum(half[i][k] * rot[j][k] for k in range(3)) + rp[i] * tr[j] + tr[i] * m1[j]
        m2[j, i] = m2[i, j]
    world = m1 + [m2[0, 0], m2[1, 1], m2[2, 2], m2[0, 1], m2[0, 2], m2[1, 2], jnp.ones((ROWS, LANES), F32)]
    for f in range(16):
        tab_ref[pl.ds(f, ROWS, stride=16), :] = world[f] if f < 10 else zeros

    nt = (((1,), (1,)), ((), ()))
    sums = jnp.zeros((48, VOX), F32)
    for t in range(TM):
        sums = sums + lax.dot_general(
            split3(wide(tab_ref, t, 16)), vhot_ref[:, t * 512 : (t + 1) * 512], nt, preferred_element_type=F32
        )
    sums = fold3(sums)
    count = jnp.maximum(sums[9:10] * PTS, 1.0)
    angles = angles_ref[...]
    cos, sin = jnp.cos(angles), jnp.sin(angles)
    n = [sin[0:1] * cos[1:2], sin[0:1] * sin[1:2], cos[0:1]]
    offset = (n[0] * sums[0:1] + n[1] * sums[1:2] + n[2] * sums[2:3]) / count
    quadric = (
        n[0] * n[0] * sums[3:4]
        + n[1] * n[1] * sums[4:5]
        + n[2] * n[2] * sums[5:6]
        + 2.0 * (n[0] * n[1] * sums[6:7] + n[0] * n[2] * sums[7:8] + n[1] * n[2] * sums[8:9])
    )
    cost_ref[...] = quadric / count - offset * offset
    plane = split3(jnp.concatenate(n + [offset, jnp.zeros((4, VOX), F32)], axis=0))
    for t in range(TM):
        got = jnp.dot(plane, vhot_ref[:, t * 512 : (t + 1) * 512], preferred_element_type=F32)
        put(gat_ref, t, 8, fold3(got))
    n0, n1, n2, d = [gat_ref[pl.ds(f, ROWS, stride=8), :] for f in range(4)]
    nb = [n0, n1, n2]

    def cross(v):
        return [v[1] * n2 - v[2] * n1, v[2] * n0 - v[0] * n2, v[0] * n1 - v[1] * n0]

    am2 = list(zip(*[cross([m2[0, j], m2[1, j], m2[2, j]]) for j in range(3)]))
    ama = [cross(am2[i]) for i in range(3)]
    am1 = cross(m1)
    terms = {}
    for i in range(3):
        for j in range(i, 3):
            terms[i, j] = ama[i][j]
            terms[3 + i, 3 + j] = PTS * nb[i] * nb[j]
        for j in range(3):
            terms[i, 3 + j] = am1[i] * nb[j]
    resid = sum(nb[i] * m1[i] for i in range(3)) - PTS * d
    grad = [sum(am2[i][j] * nb[j] for j in range(3)) - d * am1[i] for i in range(3)] + [nb[i] * resid for i in range(3)]
    features = [terms[i, j] for i in range(6) for j in range(i, 6)] + grad
    for f in range(32):
        feat_ref[pl.ds(f, ROWS, stride=32), :] = features[f] if f < 27 else zeros
    for t in range(TM):
        ft = wide(feat_ref, t, 32)
        hi = ft.astype(BF16)
        lo = (ft - hi.astype(F32)).astype(BF16)
        got = lax.dot_general(jnp.concatenate([hi, lo], axis=0), hot_ref[t], nt, preferred_element_type=F32)
        got = got[:32] + got[32:]
        for c in range(4):
            part = [got[8 * j : 8 * j + 8, c * LANES : (c + 1) * LANES] for j in range(4)]
            for g, v in enumerate(swap_groups(part)):
                out_ref[t * 16 + 4 * c + g] = v


def scans_kernel(scale, recv_ref, hess_ref, grad_ref):
    total = jnp.sum(recv_ref[...], axis=0) * scale
    part = [total[:, j * SLOTS : (j + 1) * SLOTS] for j in range(4)]
    f = 0
    for i in range(6):
        for j in range(i, 6):
            row = part[f // 8][f % 8 : f % 8 + 1]
            hess_ref[6 * i + j : 6 * i + j + 1, :] = row
            if i != j:
                hess_ref[6 * j + i : 6 * j + i + 1, :] = row
            f += 1
    for i in range(6):
        grad_ref[i : i + 1, :] = part[f // 8][f % 8 : f % 8 + 1]
        f += 1


def local(points, poses, normal_angles, voxel_ids, scan_ids):
    axes = ("tm", "map")
    blocks = points.shape[1]
    devices = lax.axis_size(axes)
    steps = 8
    sent = pl.pallas_call(
        moments_kernel,
        grid=(steps,),
        in_specs=[
            pl.BlockSpec((3, blocks // steps, PTS), lambda i: (0, i, 0)),
            pl.BlockSpec((ROWS, LANES), lambda i: (0, 0)),
            pl.BlockSpec((ROWS, LANES), lambda i: (0, 0)),
            pl.BlockSpec((6, SLOTS), lambda i: (0, 0)),
        ],
        out_specs=pl.BlockSpec((devices * SENT_ROWS, LANES), lambda i: (0, 0)),
        out_shape=jax.ShapeDtypeStruct((devices * SENT_ROWS, LANES), F32),
        scratch_shapes=[pltpu.VMEM((9, ROWS, LANES), F32)],
        compiler_params=pltpu.CompilerParams(vmem_limit_bytes=32 * 1024 * 1024),
    )(points, voxel_ids.reshape(ROWS, LANES), scan_ids.reshape(ROWS, LANES), poses)
    recv = lax.all_to_all(sent.reshape(devices, 1, SENT_ROWS * LANES), axes, 0, 0, tiled=True)
    recv = recv.reshape(devices * SENT_ROWS, LANES)
    shares, cost = pl.pallas_call(
        owner_kernel,
        out_shape=(
            jax.ShapeDtypeStruct((devices, 8, LANES), F32),
            jax.ShapeDtypeStruct((1, VOX), F32),
        ),
        scratch_shapes=[
            pltpu.VMEM((ROWS * 16, LANES), F32),
            pltpu.VMEM((ROWS * 16, LANES), F32),
            pltpu.VMEM((TM, SCAN_ROW, 512), BF16),
            pltpu.VMEM((VOX, 4096), BF16),
            pltpu.VMEM((ROWS * 32, LANES), F32),
        ],
        compiler_params=pltpu.CompilerParams(vmem_limit_bytes=32 * 1024 * 1024),
    )(recv, normal_angles)
    arrived = lax.all_to_all(shares, axes, 0, 0, tiled=True)
    all_scans = poses.shape[1] * devices
    scale = all_scans / (blocks * devices * PTS)
    hess, grad = pl.pallas_call(
        functools.partial(scans_kernel, scale),
        out_shape=(
            jax.ShapeDtypeStruct((36, SLOTS), F32),
            jax.ShapeDtypeStruct((6, SLOTS), F32),
        ),
    )(arrived)
    return hess, grad, cost.reshape(VOX)


def solution(mesh):
    return jax.shard_map(
        local,
        mesh=mesh,
        in_specs=(
            P(None, ("tm", "map"), None),
            P(None, ("tm", "map")),
            P(None, ("tm", "map")),
            P(("tm", "map")),
            P(("tm", "map")),
        ),
        out_specs=(P(None, ("tm", "map")), P(None, ("tm", "map")), P(("tm", "map"))),
        check_vma=False,
    )
```

profile of v0, /device:TPU:1, one launch (start us, length us, event | category | flops | bytes accessed | tf_op | source)
XLA Modules:
  0.0 58.1 jit_solution(10695156106601755830)
XLA Ops:
  0.6 0.0 copy-start.4
  0.6 0.0 copy-start
  0.7 2.8 %copy-done = f32[3,4096,128]{2,1,0:T(8,128)S(1)} copy-done((f32[3,4096,128]{2,1,0:T(8,128)S(1)}, f32[3,4096,128]{2,1,0:T(8,128)}, u32[]{:S(2)}) %copy-start) | copy-done | bytes 6291480
  3.4 0.0 copy-start.1
  3.4 0.7 %copy-done.1 = s32[4096]{0:T(1024)S(1)} copy-done((s32[4096]{0:T(1024)S(1)}, s32[4096]{0:T(1024)}, u32[]{:S(2)}) %copy-start.1) | copy-done | bytes 16408
  4.2 0.0 copy-start.2
  4.2 0.7 %copy-done.2 = s32[4096]{0:T(1024)S(1)} copy-done((s32[4096]{0:T(1024)S(1)}, s32[4096]{0:T(1024)}, u32[]{:S(2)}) %copy-start.2) | copy-done | bytes 16408
  4.9 0.0 copy-start.3
  4.9 0.7 %copy-done.3 = f32[6,32]{1,0:T(8,128)S(1)} copy-done((f32[6,32]{1,0:T(8,128)S(1)}, f32[6,32]{1,0:T(8,128)}, u32[]{:S(2)}) %copy-start.3) | copy-done | bytes 792
  5.6 3.0 %shard_map.76 = f32[640,128]{1,0:T(8,128)S(1)} custom-call(f32[3,4096,128]{2,1,0:T(8,128)S(1)} %copy-done, s32[32,128]{1,0:T(8,128)S(1)} %bitcast.7, s32[32,128]{1,0:T(8,128)S(1)} %bitcast.8, f32[6,32]{1,0:T(8,128)S(1)} %copy-done.3), custom_call_target="tpu_custom_call" | custom-call | tf_op jit(solution)/shard_map/pallas_call | solution.py:227
  8.5 22.7 %all_to_all.10 = f32[128,1,640]{2,1,0:T(1,128)S(1)} all-to-all(f32[128,1,640]{2,1,0:T(1,128)S(1)} %bitcast.5), channel_id=1, replica_groups=mesh['tm'=8,'map'=16] {'tm','map'}, dimensions={0} | all-to-all | bytes 655360 | tf_op jit(solution)/shard_map/all_to_all | solution.py:241
  31.2 0.0 copy-done.4
  31.2 5.5 %shard_map.77 = (f32[128,8,128]{2,1,0:T(8,128)S(1)}, f32[1,256]{1,0:T(1,128)}) custom-call(f32[640,128]{1,0:T(8,128)S(1)} %bitcast.6, f32[2,256]{1,0:T(2,128)S(1)} %copy-done.4), custom_call_target="tpu_custom_call" | custom-call | tf_op jit(solution)/shard_map/pallas_call | solution.py:243
  36.7 18.2 %all_to_all.11.recv_ref = f32[128,8,128]{2,1,0:T(8,128)} all-to-all(f32[128,8,128]{2,1,0:T(8,128)S(1)} %get-tuple-element.7), channel_id=1, replica_groups=mesh['tm'=8,'map'=16] {'tm','map'}, dimensions={0} | all-to-all | bytes 1048576 | tf_op jit(solution)/shard_map/all_to_all | solution.py:258
  54.9 1.9 %shard_map.78 = (f32[36,32]{1,0:T(8,128)}, f32[6,32]{1,0:T(8,128)}) custom-call(f32[128,8,128]{2,1,0:T(8,128)} %all_to_all.11.recv_ref), custom_call_target="tpu_custom_call" | custom-call | tf_op jit(solution)/shard_map/pallas_call | solution.py:261
  56.7 1.4 %copy.10 = f32[36,32]{0,1:T(8,128)} copy(f32[36,32]{1,0:T(8,128)} %get-tuple-element.14) | data formatting | bytes 9216
Async XLA Ops:
  0.6 30.6 %copy-start.4 = (f32[2,256]{1,0:T(2,128)S(1)}, f32[2,256]{1,0:T(2,128)}, u32[]{:S(2)}) copy-start(f32[2,256]{1,0:T(2,128)} %angles_ref.1) | copy-start | bytes 6148
  0.6 2.8 %copy-start = (f32[3,4096,128]{2,1,0:T(8,128)S(1)}, f32[3,4096,128]{2,1,0:T(8,128)}, u32[]{:S(2)}) copy-start(f32[3,4096,128]{2,1,0:T(8,128)} %points_ref.1) | copy-start | bytes 18874372
  3.4 0.7 %copy-start.1 = (s32[4096]{0:T(1024)S(1)}, s32[4096]{0:T(1024)}, u32[]{:S(2)}) copy-start(s32[4096]{0:T(1024)} %param.8) | copy-start | bytes 49156
  4.2 0.7 %copy-start.2 = (s32[4096]{0:T(1024)S(1)}, s32[4096]{0:T(1024)}, u32[]{:S(2)}) copy-start(s32[4096]{0:T(1024)} %param.9) | copy-start | bytes 49156
  4.9 0.7 %copy-start.3 = (f32[6,32]{1,0:T(8,128)S(1)}, f32[6,32]{1,0:T(8,128)}, u32[]{:S(2)}) copy-start(f32[6,32]{1,0:T(8,128)} %poses_ref.1) | copy-start | bytes 2308
where the time goes:
time: 58.5 us; the launch traced here: 58.1 us
  blocking collectives  40.9 us (70%)
  Pallas kernels  10.3 us (18%)
  local copies, waits for them, and re-layouts  6.32 us (11%)
  between operations  0.67 us (1%)
    all_to_all x1, blocking collectives, local(): lax.all_to_all(sent.reshape(devices, 1, SENT_ROWS * LANES), axes, 0, 0, t...  22.7 us
    all_to_all x1, blocking collectives, local(): arrived = lax.all_to_all(shares, axes, 0, 0, tiled=True)  18.2 us
    unnamed x11, local copies, waits for them, and re-layouts  6.32 us
    pallas_call x1, Pallas kernels, local(): pl.pallas_call(owner_kernel, out_shape=(jax.ShapeDtypeStruct((devices, 8,...  5.47 us
    pallas_call x1, Pallas kernels, local(): pl.pallas_call(moments_kernel, grid=(steps,), in_specs=[pl.BlockSpec((3,...  2.96 us
    pallas_call x1, Pallas kernels, local(): pl.pallas_call(functools.partial(scans_kernel, scale), out_shape=(jax.Sha...  1.85 us

commit v1 on v0

--- a/solution.py
+++ b/solution.py
@@ -46,46 +46,64 @@
     return x[:n] + x[n : 2 * n] + x[2 * n :]
 
 
-def moments_kernel(points_ref, vox_ref, scan_ref, poses_ref, sent_ref, acc_ref):
-    step = pl.program_id(0)
-    chunks = points_ref.shape[1] // LANES
-    for cc in range(chunks):
-        span = pl.ds(cc * LANES, LANES)
-        x = points_ref[0, span, :].T
-        y = points_ref[1, span, :].T
-        z = points_ref[2, span, :].T
-        quantities = [x, y, z, x * x, y * y, z * z, x * y, x * z, y * z]
-        for f, q in enumerate(quantities):
-            acc_ref[f, pl.ds(step * chunks + cc, 1), :] = jnp.sum(q, axis=0, keepdims=True)
-
-    @pl.when(step == pl.num_programs(0) - 1)
-    def _():
-        lane = lax.broadcasted_iota(jnp.int32, (ROWS, LANES), 1)
-        row = lax.broadcasted_iota(jnp.int32, (ROWS, LANES), 0)
-        vox = vox_ref[...]
-        owner = row * GROUPS + lane // SLOTS
-        vox = jnp.where(vox >= 0, vox - owner * VOX, -1).astype(F32)
-        scan = scan_ref[...].astype(F32)
-        p = poses_ref[...]
-        p = jnp.concatenate([p, p, p, p], axis=1)
-        cos, sin = jnp.cos(p[:3]), jnp.sin(p[:3])
-        one = [cos[0:1], sin[0:1], cos[1:2], sin[1:2], cos[2:3], sin[2:3], p[3:4], p[4:5], p[5:6]]
-        group = lax.broadcasted_iota(jnp.int32, (1, LANES), 1) // SLOTS
-        f = [acc_ref[i] for i in range(9)]
-        whole = lambda r: jnp.broadcast_to(r, (ROWS, LANES))
-        k0 = swap_groups(f[0:4])
-        k1 = swap_groups(f[4:8])
-        k2 = swap_groups([f[8], vox, scan, whole(one[0])])
-
-        def four(rs):
-            r = jnp.where(group == 0, rs[0], jnp.where(group == 1, rs[1], jnp.where(group == 2, rs[2], rs[3])))
-            return whole(r)
-
-        k3 = four(one[1:5])
-        k4 = four(one[5:9])
-        for g in range(GROUPS):
-            for k, v in enumerate([k0[g], k1[g], k2[g], k3, k4]):
-                sent_ref[pl.ds(g * SENT_ROWS + k, ROWS, stride=GROUPS * SENT_ROWS), :] = v
+def moments_kernel(points_hbm, vox_hbm, scan_hbm, poses_hbm, sent_ref, acc_ref, points_ref, vox_ref, scan_ref, poses_ref, sems, small_sems):
+    chunks = sems.shape[0]
+    size = points_ref.shape[1] // chunks
+
+    def fetch(c):
+        span = pl.ds(c * size, size)
+        return pltpu.make_async_copy(points_hbm.at[:, span, :], points_ref.at[:, span, :], sems.at[c])
+
+    small = [
+        pltpu.make_async_copy(vox_hbm, vox_ref, small_sems.at[0]),
+        pltpu.make_async_copy(scan_hbm, scan_ref, small_sems.at[1]),
+        pltpu.make_async_copy(poses_hbm, poses_ref, small_sems.at[2]),
+    ]
+    for c in range(chunks):
+        fetch(c).start()
+    for copy in small:
+        copy.start()
+
+    @pl.loop(0, chunks)
+    def _(c):
+        fetch(c).wait()
+        for cc in range(size // LANES):
+            span = pl.ds(pl.multiple_of(c * size + cc * LANES, LANES), LANES)
+            x = points_ref[0, span, :].T
+            y = points_ref[1, span, :].T
+            z = points_ref[2, span, :].T
+            quantities = [x, y, z, x * x, y * y, z * z, x * y, x * z, y * z]
+            for f, q in enumerate(quantities):
+                acc_ref[f, pl.ds(c * (size // LANES) + cc, 1), :] = jnp.sum(q, axis=0, keepdims=True)
+
+    for copy in small:
+        copy.wait()
+    lane = lax.broadcasted_iota(jnp.int32, (ROWS, LANES), 1)
+    row = lax.broadcasted_iota(jnp.int32, (ROWS, LANES), 0)
+    vox = vox_ref[...]
+    owner = row * GROUPS + lane // SLOTS
+    vox = jnp.where(vox >= 0, vox - owner * VOX, -1).astype(F32)
+    scan = scan_ref[...].astype(F32)
+    p = poses_ref[...]
+    p = jnp.concatenate([p, p, p, p], axis=1)
+    cos, sin = jnp.cos(p[:3]), jnp.sin(p[:3])
+    one = [cos[0:1], sin[0:1], cos[1:2], sin[1:2], cos[2:3], sin[2:3], p[3:4], p[4:5], p[5:6]]
+    group = lax.broadcasted_iota(jnp.int32, (1, LANES), 1) // SLOTS
+    f = [acc_ref[i] for i in range(9)]
+    whole = lambda r: jnp.broadcast_to(r, (ROWS, LANES))
+    k0 = swap_groups(f[0:4])
+    k1 = swap_groups(f[4:8])
+    k2 = swap_groups([f[8], vox, scan, whole(one[0])])
+
+    def four(rs):
+        r = jnp.where(group == 0, rs[0], jnp.where(group == 1, rs[1], jnp.where(group == 2, rs[2], rs[3])))
+        return whole(r)
+
+    k3 = four(one[1:5])
+    k4 = four(one[5:9])
+    for g in range(GROUPS):
+        for k, v in enumerate([k0[g], k1[g], k2[g], k3, k4]):
+            sent_ref[pl.ds(g * SENT_ROWS + k, ROWS, stride=GROUPS * SENT_ROWS), :] = v
 
 
 def owner_kernel(recv_ref, angles_ref, out_ref, cost_ref, tab_ref, gat_ref, hot_ref, vhot_ref, feat_ref):
@@ -206,37 +224,33 @@
 def scans_kernel(scale, recv_ref, hess_ref, grad_ref):
     total = jnp.sum(recv_ref[...], axis=0) * scale
     part = [total[:, j * SLOTS : (j + 1) * SLOTS] for j in range(4)]
-    f = 0
-    for i in range(6):
-        for j in range(i, 6):
-            row = part[f // 8][f % 8 : f % 8 + 1]
-            hess_ref[6 * i + j : 6 * i + j + 1, :] = row
-            if i != j:
-                hess_ref[6 * j + i : 6 * j + i + 1, :] = row
-            f += 1
-    for i in range(6):
-        grad_ref[i : i + 1, :] = part[f // 8][f % 8 : f % 8 + 1]
-        f += 1
+    rows = [part[f // 8][f % 8 : f % 8 + 1] for f in range(27)]
+    place = {ij: f for f, ij in enumerate([(i, j) for i in range(6) for j in range(i, 6)])}
+    hess = [rows[place[min(i, j), max(i, j)]] for i in range(6) for j in range(6)]
+    hess_ref[...] = jnp.concatenate(hess, axis=0).T
+    grad_ref[...] = jnp.concatenate(rows[21:], axis=0)
 
 
 def local(points, poses, normal_angles, voxel_ids, scan_ids):
     axes = ("tm", "map")
     blocks = points.shape[1]
     devices = lax.axis_size(axes)
-    steps = 8
+    anywhere = pl.BlockSpec(memory_space=pl.ANY)
+    chunks = 8
     sent = pl.pallas_call(
         moments_kernel,
-        grid=(steps,),
-        in_specs=[
-            pl.BlockSpec((3, blocks // steps, PTS), lambda i: (0, i, 0)),
-            pl.BlockSpec((ROWS, LANES), lambda i: (0, 0)),
-            pl.BlockSpec((ROWS, LANES), lambda i: (0, 0)),
-            pl.BlockSpec((6, SLOTS), lambda i: (0, 0)),
+        in_specs=[anywhere] * 4,
+        out_shape=jax.ShapeDtypeStruct((devices * SENT_ROWS, LANES), F32),
+        scratch_shapes=[
+            pltpu.VMEM((9, ROWS, LANES), F32),
+            pltpu.VMEM(points.shape, F32),
+            pltpu.VMEM((ROWS, LANES), jnp.int32),
+            pltpu.VMEM((ROWS, LANES), jnp.int32),
+            pltpu.VMEM(poses.shape, F32),
+            pltpu.SemaphoreType.DMA((chunks,)),
+            pltpu.SemaphoreType.DMA((3,)),
         ],
-        out_specs=pl.BlockSpec((devices * SENT_ROWS, LANES), lambda i: (0, 0)),
-        out_shape=jax.ShapeDtypeStruct((devices * SENT_ROWS, LANES), F32),
-        scratch_shapes=[pltpu.VMEM((9, ROWS, LANES), F32)],
-        compiler_params=pltpu.CompilerParams(vmem_limit_bytes=32 * 1024 * 1024),
+        compiler_params=pltpu.CompilerParams(vmem_limit_bytes=56 * 1024 * 1024),
     )(points, voxel_ids.reshape(ROWS, LANES), scan_ids.reshape(ROWS, LANES), poses)
     recv = lax.all_to_all(sent.reshape(devices, 1, SENT_ROWS * LANES), axes, 0, 0, tiled=True)
     recv = recv.reshape(devices * SENT_ROWS, LANES)
@@ -261,11 +275,12 @@
     hess, grad = pl.pallas_call(
         functools.partial(scans_kernel, scale),
         out_shape=(
-            jax.ShapeDtypeStruct((36, SLOTS), F32),
+            jax.ShapeDtypeStruct((SLOTS, 36), F32),
             jax.ShapeDtypeStruct((6, SLOTS), F32),
         ),
+        compiler_params=pltpu.CompilerParams(vmem_limit_bytes=8 * 1024 * 1024),
     )(arrived)
-    return hess, grad, cost.reshape(VOX)
+    return hess.T, grad, cost.reshape(VOX)
 
 
 def solution(mesh):

time: 58.5 us -> 52.3 us (0.89)
  local copies, waits for them, and re-layouts: 6.32 us -> 0.01 us
    unnamed x11 -> x2, local copies, waits for them, and re-layouts: 6.32 us -> 0.01 us
    pallas_call x1, Pallas kernels: 2.96 us -> 4.41 us  [local(): pl.pallas_call(moments_kernel, in_specs=[anywhere] * 4, out_shape=jax.Sha...]
    pallas_call x1, Pallas kernels: 1.85 us -> 0.89 us  [local(): pl.pallas_call(functools.partial(scans_kernel, scale), out_shape=(jax.Sha...]
where the time goes in v1:
time: 52.3 us; the launch traced here: 52.2 us
  blocking collectives  40.7 us (78%)
  Pallas kernels  10.8 us (21%)
  between operations  0.66 us (1%)
    all_to_all x1, blocking collectives, local(): lax.all_to_all(sent.reshape(devices, 1, SENT_ROWS * LANES), axes, 0, 0, t...  22.9 us
    all_to_all x1, blocking collectives, local(): arrived = lax.all_to_all(shares, axes, 0, 0, tiled=True)  17.8 us
    pallas_call x1, Pallas kernels, local(): pl.pallas_call(owner_kernel, out_shape=(jax.ShapeDtypeStruct((devices, 8,...  5.47 us
    pallas_call x1, Pallas kernels, local(): pl.pallas_call(moments_kernel, in_specs=[anywhere] * 4, out_shape=jax.Sha...  4.41 us

profile of v1, /device:TPU:1, one launch (start us, length us, event | category | flops | bytes accessed | tf_op | source)
XLA Modules:
  0.0 52.2 jit_solution(15145892332173387287)
XLA Ops:
  0.6 0.0 copy-start
  0.6 4.4 %shard_map.76 = f32[640,128]{1,0:T(8,128)} custom-call(f32[3,4096,128]{2,1,0:T(8,128)} %points_hbm.1, s32[32,128]{1,0:T(8,128)} %bitcast.8, s32[32,128]{1,0:T(8,128)} %bitcast.9, f32[6,32]{1,0:T(8,128)} %poses_hbm.1), custom_call_target="tpu_custom_call" | custom-call | tf_op jit(solution)/shard_map/pallas_call | solution.py:240
  5.1 22.9 %all_to_all.10 = f32[128,1,640]{2,1,0:T(1,128)S(1)} all-to-all(f32[128,1,640]{2,1,0:T(1,128)} %bitcast.7), channel_id=1, replica_groups=mesh['tm'=8,'map'=16] {'tm','map'}, dimensions={0} | all-to-all | bytes 655360 | tf_op jit(solution)/shard_map/all_to_all | solution.py:255
  27.9 0.0 copy-done
  27.9 5.5 %shard_map.77 = (f32[128,8,128]{2,1,0:T(8,128)S(1)}, f32[1,256]{1,0:T(1,128)}) custom-call(f32[640,128]{1,0:T(8,128)S(1)} %bitcast.6, f32[2,256]{1,0:T(2,128)S(1)} %copy-done), custom_call_target="tpu_custom_call" | custom-call | tf_op jit(solution)/shard_map/pallas_call | solution.py:257
  33.4 17.8 %all_to_all.11.recv_ref = f32[128,8,128]{2,1,0:T(8,128)S(1)} all-to-all(f32[128,8,128]{2,1,0:T(8,128)S(1)} %get-tuple-element.7), channel_id=1, replica_groups=mesh['tm'=8,'map'=16] {'tm','map'}, dimensions={0} | all-to-all | bytes 1048576 | tf_op jit(solution)/shard_map/all_to_all | solution.py:272
  51.3 0.9 %shard_map.78 = (f32[32,36]{1,0:T(8,128)}, f32[6,32]{1,0:T(8,128)}) custom-call(f32[128,8,128]{2,1,0:T(8,128)S(1)} %all_to_all.11.recv_ref), custom_call_target="tpu_custom_call" | custom-call | tf_op jit(solution)/shard_map/pallas_call | solution.py:275
Async XLA Ops:
  0.6 27.3 %copy-start = (f32[2,256]{1,0:T(2,128)S(1)}, f32[2,256]{1,0:T(2,128)}, u32[]{:S(2)}) copy-start(f32[2,256]{1,0:T(2,128)} %angles_ref.1) | copy-start | bytes 6148

commit v2 on v1

--- a/solution.py
+++ b/solution.py
@@ -12,6 +12,7 @@
 SLOTS = 32
 PTS = 128
 SENT_ROWS = 5
+BACK_ROWS = 7
 ROWS = 32
 TM = 8
 SCAN_ROW = 512
@@ -106,7 +107,25 @@
             sent_ref[pl.ds(g * SENT_ROWS + k, ROWS, stride=GROUPS * SENT_ROWS), :] = v
 
 
-def owner_kernel(recv_ref, angles_ref, out_ref, cost_ref, tab_ref, gat_ref, hot_ref, vhot_ref, feat_ref):
+def one_hot(condition):
+    return jnp.where(condition, 1.0, 0.0).astype(BF16)
+
+
+def hot16(iota, ids):
+    return jnp.where(iota == ids, jnp.ones_like(iota), jnp.zeros_like(iota))
+
+
+def look_up(table, index):
+    low = index % LANES
+    high = index // LANES
+    out = None
+    for k, part in enumerate(table):
+        got = jnp.take_along_axis(part, low, axis=1, mode="promise_in_bounds")
+        out = got if out is None else jnp.where(high == k, got, out)
+    return out
+
+
+def owner_kernel(recv_ref, angles_ref, out_ref, cost_ref, tab_ref, gat_ref, feat_ref):
     feats = []
     for k in range(SENT_ROWS):
         rows = [recv_ref[pl.ds(h * SENT_ROWS + k, ROWS, stride=GROUPS * SENT_ROWS), :] for h in range(GROUPS)]
@@ -137,19 +156,13 @@
     def wide(ref, t, n):
         return jnp.concatenate([ref[pl.ds((t * 4 + i) * n, n), :] for i in range(4)], axis=1)
 
-    def put(ref, t, n, val):
-        for i in range(4):
-            ref[pl.ds((t * 4 + i) * n, n), :] = val[:, i * LANES : (i + 1) * LANES]
-
-    scan_iota = lax.broadcasted_iota(jnp.int32, (SCAN_ROW, LANES), 0)
-    vox_iota = lax.broadcasted_iota(jnp.int32, (VOX, LANES), 0)
     for t in range(TM):
-        for i in range(4):
-            r = 4 * t + i
-            hot_ref[t, :, i * LANES : (i + 1) * LANES] = jnp.where(scan_iota == scan[r : r + 1, :], 1.0, 0.0).astype(BF16)
-            vhot_ref[:, r * LANES : (r + 1) * LANES] = jnp.where(vox_iota == vox[r : r + 1, :], 1.0, 0.0).astype(BF16)
-        got = jnp.dot(split3(wide(tab_ref, t, 16)), hot_ref[t], preferred_element_type=F32)
-        put(gat_ref, t, 16, fold3(got))
+        for half in range(2):
+            parts = [tab_ref[pl.ds((4 * t + i) * 16 + 8 * half, 8), :] for i in range(4)]
+            for i in range(4):
+                r = 4 * t + i
+                index = jnp.broadcast_to(scan[r : r + 1, :], (8, LANES))
+                gat_ref[pl.ds(r * 16 + 8 * half, 8), :] = look_up(parts, index)
 
     rot = [[gat_ref[pl.ds(3 * i + j, ROWS, stride=16), :] for j in range(3)] for i in range(3)]
     tr = [gat_ref[pl.ds(9 + i, ROWS, stride=16), :] for i in range(3)]
@@ -166,11 +179,12 @@
         tab_ref[pl.ds(f, ROWS, stride=16), :] = world[f] if f < 10 else zeros
 
     nt = (((1,), (1,)), ((), ()))
+    vox_iota = lax.broadcasted_iota(jnp.int32, (VOX, LANES), 0).astype(F32).astype(BF16)
+    vox16 = vox.astype(F32).astype(BF16)
     sums = jnp.zeros((48, VOX), F32)
     for t in range(TM):
-        sums = sums + lax.dot_general(
-            split3(wide(tab_ref, t, 16)), vhot_ref[:, t * 512 : (t + 1) * 512], nt, preferred_element_type=F32
-        )
+        hot = jnp.concatenate([hot16(vox_iota, vox16[r : r + 1, :]) for r in range(4 * t, 4 * t + 4)], axis=1)
+        sums = sums + lax.dot_general(split3(wide(tab_ref, t, 16)), hot, nt, preferred_element_type=F32)
     sums = fold3(sums)
     count = jnp.maximum(sums[9:10] * PTS, 1.0)
     angles = angles_ref[...]
@@ -184,11 +198,14 @@
         + 2.0 * (n[0] * n[1] * sums[6:7] + n[0] * n[2] * sums[7:8] + n[1] * n[2] * sums[8:9])
     )
     cost_ref[...] = quadric / count - offset * offset
-    plane = split3(jnp.concatenate(n + [offset, jnp.zeros((4, VOX), F32)], axis=0))
-    for t in range(TM):
-        got = jnp.dot(plane, vhot_ref[:, t * 512 : (t + 1) * 512], preferred_element_type=F32)
-        put(gat_ref, t, 8, fold3(got))
-    n0, n1, n2, d = [gat_ref[pl.ds(f, ROWS, stride=8), :] for f in range(4)]
+    plane = jnp.concatenate(n + [offset] + n + [offset], axis=0)
+    parts = [plane[:, k * LANES : (k + 1) * LANES] for k in range(VOX // LANES)]
+    sub = lax.broadcasted_iota(jnp.int32, (8, LANES), 0)
+    for r in range(0, ROWS, 2):
+        index = jnp.where(sub < 4, vox[r : r + 1, :], vox[r + 1 : r + 2, :])
+        got = look_up(parts, jnp.maximum(index, 0))
+        gat_ref[pl.ds(r * 4, 8), :] = jnp.where(index >= 0, got, 0.0)
+    n0, n1, n2, d = [gat_ref[pl.ds(f, ROWS, stride=4), :] for f in range(4)]
     nb = [n0, n1, n2]
 
     def cross(v):
@@ -207,37 +224,49 @@
     resid = sum(nb[i] * m1[i] for i in range(3)) - PTS * d
     grad = [sum(am2[i][j] * nb[j] for j in range(3)) - d * am1[i] for i in range(3)] + [nb[i] * resid for i in range(3)]
     features = [terms[i, j] for i in range(6) for j in range(i, 6)] + grad
-    for f in range(32):
-        feat_ref[pl.ds(f, ROWS, stride=32), :] = features[f] if f < 27 else zeros
+    for row in range(32):
+        f = row % 8 * 4 + row // 8
+        feat_ref[pl.ds(row, ROWS, stride=32), :] = features[f] if f < 27 else zeros
+
+    high = [one_hot(scan >= 256) if k else one_hot(scan < 256) for k in range(2)]
+    low = (scan % 256).astype(F32).T.astype(BF16)
+    scan_iota = lax.broadcasted_iota(jnp.int32, (LANES, 256), 1).astype(F32).astype(BF16)
     for t in range(TM):
         ft = wide(feat_ref, t, 32)
         hi = ft.astype(BF16)
         lo = (ft - hi.astype(F32)).astype(BF16)
-        got = lax.dot_general(jnp.concatenate([hi, lo], axis=0), hot_ref[t], nt, preferred_element_type=F32)
-        got = got[:32] + got[32:]
+        both = jnp.concatenate([hi, lo], axis=0)
+        masks = [jnp.concatenate([h[r : r + 1, :] for r in range(4 * t, 4 * t + 4)], axis=1) for h in high]
+        left = jnp.concatenate([both * m for m in masks], axis=0)
+        hot = jnp.concatenate([hot16(scan_iota, low[:, r : r + 1]) for r in range(4 * t, 4 * t + 4)], axis=0)
+        got = jnp.dot(left, hot, preferred_element_type=F32)
         for c in range(4):
-            part = [got[8 * j : 8 * j + 8, c * LANES : (c + 1) * LANES] for j in range(4)]
+            top = 64 * (c // 2)
+            lanes = slice(c % 2 * LANES, (c % 2 + 1) * LANES)
+            sums_c = got[top : top + 32, lanes] + got[top + 32 : top + 64, lanes]
+            part = [sums_c[8 * j : 8 * j + 8] for j in range(4)]
             for g, v in enumerate(swap_groups(part)):
-                out_ref[t * 16 + 4 * c + g] = v
+                out_ref[pl.ds((t * 16 + 4 * c + g) * BACK_ROWS, BACK_ROWS), :] = v[:BACK_ROWS]
 
 
 def scans_kernel(scale, recv_ref, hess_ref, grad_ref):
-    total = jnp.sum(recv_ref[...], axis=0) * scale
+    eight = 8 * BACK_ROWS
+    acc = recv_ref[0:eight, :]
+    for q in range(1, recv_ref.shape[0] // eight):
+        acc = acc + recv_ref[q * eight : (q + 1) * eight, :]
+    total = sum(acc[q * BACK_ROWS : (q + 1) * BACK_ROWS] for q in range(8)) * scale
     part = [total[:, j * SLOTS : (j + 1) * SLOTS] for j in range(4)]
-    rows = [part[f // 8][f % 8 : f % 8 + 1] for f in range(27)]
+    rows = [part[f % 4][f // 4 : f // 4 + 1] for f in range(27)]
     place = {ij: f for f, ij in enumerate([(i, j) for i in range(6) for j in range(i, 6)])}
     hess = [rows[place[min(i, j), max(i, j)]] for i in range(6) for j in range(6)]
     hess_ref[...] = jnp.concatenate(hess, axis=0).T
     grad_ref[...] = jnp.concatenate(rows[21:], axis=0)
 
 
-def local(points, poses, normal_angles, voxel_ids, scan_ids):
-    axes = ("tm", "map")
-    blocks = points.shape[1]
-    devices = lax.axis_size(axes)
+def moments(points, voxel_ids, scan_ids, poses, devices):
     anywhere = pl.BlockSpec(memory_space=pl.ANY)
     chunks = 8
-    sent = pl.pallas_call(
+    return pl.pallas_call(
         moments_kernel,
         in_specs=[anywhere] * 4,
         out_shape=jax.ShapeDtypeStruct((devices * SENT_ROWS, LANES), F32),
@@ -252,24 +281,34 @@
         ],
         compiler_params=pltpu.CompilerParams(vmem_limit_bytes=56 * 1024 * 1024),
     )(points, voxel_ids.reshape(ROWS, LANES), scan_ids.reshape(ROWS, LANES), poses)
-    recv = lax.all_to_all(sent.reshape(devices, 1, SENT_ROWS * LANES), axes, 0, 0, tiled=True)
-    recv = recv.reshape(devices * SENT_ROWS, LANES)
-    shares, cost = pl.pallas_call(
+
+
+def owner(recv, normal_angles, devices):
+    return pl.pallas_call(
         owner_kernel,
         out_shape=(
-            jax.ShapeDtypeStruct((devices, 8, LANES), F32),
+            jax.ShapeDtypeStruct((devices * BACK_ROWS, LANES), F32),
             jax.ShapeDtypeStruct((1, VOX), F32),
         ),
         scratch_shapes=[
             pltpu.VMEM((ROWS * 16, LANES), F32),
             pltpu.VMEM((ROWS * 16, LANES), F32),
-            pltpu.VMEM((TM, SCAN_ROW, 512), BF16),
-            pltpu.VMEM((VOX, 4096), BF16),
             pltpu.VMEM((ROWS * 32, LANES), F32),
         ],
         compiler_params=pltpu.CompilerParams(vmem_limit_bytes=32 * 1024 * 1024),
     )(recv, normal_angles)
-    arrived = lax.all_to_all(shares, axes, 0, 0, tiled=True)
+
+
+def local(points, poses, normal_angles, voxel_ids, scan_ids):
+    axes = ("tm", "map")
+    blocks = points.shape[1]
+    devices = lax.axis_size(axes)
+    sent = moments(points, voxel_ids, scan_ids, poses, devices)
+    recv = lax.all_to_all(sent.reshape(devices, 1, SENT_ROWS * LANES), axes, 0, 0, tiled=True)
+    recv = recv.reshape(devices * SENT_ROWS, LANES)
+    shares, cost = owner(recv, normal_angles, devices)
+    arrived = lax.all_to_all(shares.reshape(devices, 1, BACK_ROWS * LANES), axes, 0, 0, tiled=True)
+    arrived = arrived.reshape(devices * BACK_ROWS, LANES)
     all_scans = poses.shape[1] * devices
     scale = all_scans / (blocks * devices * PTS)
     hess, grad = pl.pallas_call(

time: 52.3 us -> 48.9 us (0.935)
  Pallas kernels: 10.8 us -> 7.96 us
  blocking collectives: 40.7 us -> 40.1 us
    pallas_call x2, Pallas kernels: 9.88 us -> 7.16 us  [the longest x1 4.41 us: moments(): pl.pallas_call(moments_kernel, in_specs=[anywhere] * 4, out_shape=jax.Sha...]
    all_to_all x1, blocking collectives: 17.8 us -> 17.2 us  [local(): lax.all_to_all(shares.reshape(devices, 1, BACK_ROWS * LANES), axes, 0, 0,...]
where the time goes in v2:
time: 48.9 us; the launch traced here: 48.7 us
  blocking collectives  40.1 us (82%)
  Pallas kernels  7.96 us (16%)
  between operations  0.66 us (1%)
    all_to_all x1, blocking collectives, local(): lax.all_to_all(sent.reshape(devices, 1, SENT_ROWS * LANES), axes, 0, 0, t...  22.9 us
    all_to_all x1, blocking collectives, local(): lax.all_to_all(shares.reshape(devices, 1, BACK_ROWS * LANES), axes, 0, 0,...  17.2 us
    pallas_call x1, Pallas kernels, moments(): pl.pallas_call(moments_kernel, in_specs=[anywhere] * 4, out_shape=jax.Sha...  4.41 us
    pallas_call x1, Pallas kernels, owner(): pl.pallas_call(owner_kernel, out_shape=(jax.ShapeDtypeStruct((devices * B...  2.75 us

profile of v2, /device:TPU:1, one launch (start us, length us, event | category | flops | bytes accessed | tf_op | source)
XLA Modules:
  0.0 48.7 jit_solution(14487037430437665445)
XLA Ops:
  0.6 0.0 copy-start
  0.6 4.4 %shard_map.76 = f32[640,128]{1,0:T(8,128)} custom-call(f32[3,4096,128]{2,1,0:T(8,128)} %points_hbm.1, s32[32,128]{1,0:T(8,128)} %bitcast.12, s32[32,128]{1,0:T(8,128)} %bitcast.13, f32[6,32]{1,0:T(8,128)} %poses_hbm.1), custom_call_target="tpu_custom_call" | custom-call | tf_op jit(solution)/shard_map/pallas_call | solution.py:269
  5.1 22.9 %all_to_all.10 = f32[128,1,640]{2,1,0:T(1,128)S(1)} all-to-all(f32[128,1,640]{2,1,0:T(1,128)} %bitcast.11), channel_id=1, replica_groups=mesh['tm'=8,'map'=16] {'tm','map'}, dimensions={0} | all-to-all | bytes 655360 | tf_op jit(solution)/shard_map/all_to_all | solution.py:307
  27.9 0.0 copy-done
  27.9 2.8 %shard_map.77 = (f32[896,128]{1,0:T(8,128)S(1)}, f32[1,256]{1,0:T(1,128)}) custom-call(f32[640,128]{1,0:T(8,128)S(1)} %bitcast.9, f32[2,256]{1,0:T(2,128)S(1)} %copy-done), custom_call_target="tpu_custom_call" | custom-call | tf_op jit(solution)/shard_map/pallas_call | solution.py:287
  30.7 17.2 %all_to_all.11 = f32[128,1,896]{2,1,0:T(1,128)S(1)} all-to-all(f32[128,1,896]{2,1,0:T(1,128)S(1)} %bitcast.10), channel_id=1, replica_groups=mesh['tm'=8,'map'=16] {'tm','map'}, dimensions={0} | all-to-all | bytes 917504 | tf_op jit(solution)/shard_map/all_to_all | solution.py:310
  47.9 0.8 %shard_map.78 = (f32[32,36]{1,0:T(8,128)}, f32[6,32]{1,0:T(8,128)}) custom-call(f32[896,128]{1,0:T(8,128)S(1)} %bitcast.8), custom_call_target="tpu_custom_call" | custom-call | tf_op jit(solution)/shard_map/pallas_call | solution.py:314
Async XLA Ops:
  0.6 27.3 %copy-start = (f32[2,256]{1,0:T(2,128)S(1)}, f32[2,256]{1,0:T(2,128)}, u32[]{:S(2)}) copy-start(f32[2,256]{1,0:T(2,128)} %angles_ref.1) | copy-start | bytes 6148

commit v3 on v2

--- a/solution.py
+++ b/solution.py
@@ -87,8 +87,9 @@
     scan = scan_ref[...].astype(F32)
     p = poses_ref[...]
     p = jnp.concatenate([p, p, p, p], axis=1)
-    cos, sin = jnp.cos(p[:3]), jnp.sin(p[:3])
-    one = [cos[0:1], sin[0:1], cos[1:2], sin[1:2], cos[2:3], sin[2:3], p[3:4], p[4:5], p[5:6]]
+    half = 0.5 * p[:3]
+    tangent = jnp.sin(half) / jnp.cos(half)
+    one = [tangent[0:1], tangent[1:2], tangent[2:3], p[3:4], p[4:5], p[5:6]]
     group = lax.broadcasted_iota(jnp.int32, (1, LANES), 1) // SLOTS
     f = [acc_ref[i] for i in range(9)]
     whole = lambda r: jnp.broadcast_to(r, (ROWS, LANES))
@@ -101,7 +102,7 @@
         return whole(r)
 
     k3 = four(one[1:5])
-    k4 = four(one[5:9])
+    k4 = whole(jnp.where(group == 0, one[5], 0.0))
     for g in range(GROUPS):
         for k, v in enumerate([k0[g], k1[g], k2[g], k3, k4]):
             sent_ref[pl.ds(g * SENT_ROWS + k, ROWS, stride=GROUPS * SENT_ROWS), :] = v
@@ -134,38 +135,32 @@
     pxx, pyy, pzz, pxy, pxz, pyz = feats[3:9]
     vox = feats[9].astype(jnp.int32)
     scan = feats[10].astype(jnp.int32)
-    cx, sx, cy, sy, cz, sz, tx, ty, tz = feats[11:20]
-    table = [
-        cz * cy,
-        cz * sy * sx - sz * cx,
-        cz * sy * cx + sz * sx,
-        sz * cy,
-        sz * sy * sx + cz * cx,
-        sz * sy * cx - cz * sx,
-        -sy,
-        cy * sx,
-        cy * cx,
-        tx,
-        ty,
-        tz,
-    ]
     zeros = jnp.zeros((ROWS, LANES), F32)
-    for f in range(16):
-        tab_ref[pl.ds(f, ROWS, stride=16), :] = table[f] if f < 12 else zeros
+    for f in range(8):
+        tab_ref[pl.ds(f, ROWS, stride=8), :] = feats[11 + f] if f < 6 else zeros
 
     def wide(ref, t, n):
         return jnp.concatenate([ref[pl.ds((t * 4 + i) * n, n), :] for i in range(4)], axis=1)
 
+    scan_low = scan % LANES
+    scan_bits = [scan & LANES, scan & (2 * LANES)]
     for t in range(TM):
-        for half in range(2):
-            parts = [tab_ref[pl.ds((4 * t + i) * 16 + 8 * half, 8), :] for i in range(4)]
-            for i in range(4):
-                r = 4 * t + i
-                index = jnp.broadcast_to(scan[r : r + 1, :], (8, LANES))
-                gat_ref[pl.ds(r * 16 + 8 * half, 8), :] = look_up(parts, index)
-
-    rot = [[gat_ref[pl.ds(3 * i + j, ROWS, stride=16), :] for j in range(3)] for i in range(3)]
-    tr = [gat_ref[pl.ds(9 + i, ROWS, stride=16), :] for i in range(3)]
+        parts = [tab_ref[pl.ds((4 * t + i) * 8, 8), :] for i in range(4)]
+        for r in range(4 * t, 4 * t + 4):
+            low_index = jnp.broadcast_to(scan_low[r : r + 1, :], (8, LANES))
+            got = [jnp.take_along_axis(p, low_index, axis=1, mode="promise_in_bounds") for p in parts]
+            b0, b1 = [jnp.broadcast_to(b[r : r + 1, :], (8, LANES)) != 0 for b in scan_bits]
+            gat_ref[pl.ds(r * 8, 8), :] = jnp.where(b1, jnp.where(b0, got[3], got[2]), jnp.where(b0, got[1], got[0]))
+    pose = [gat_ref[pl.ds(f, ROWS, stride=8), :] for f in range(6)]
+    inverse = [1.0 / (1.0 + u * u) for u in pose[:3]]
+    sx, sy, sz = [2.0 * u * v for u, v in zip(pose[:3], inverse)]
+    cx, cy, cz = [(1.0 - u * u) * v for u, v in zip(pose[:3], inverse)]
+    tr = pose[3:]
+    rot = [
+        [cz * cy, cz * sy * sx - sz * cx, cz * sy * cx + sz * sx],
+        [sz * cy, sz * sy * sx + cz * cx, sz * sy * cx - cz * sx],
+        [-sy, cy * sx, cy * cx],
+    ]
     second = [[pxx, pxy, pxz], [pxy, pyy, pyz], [pxz, pyz, pzz]]
     rp = [sum(rot[i][j] * p1[j] for j in range(3)) for i in range(3)]
     half = [[sum(rot[i][k] * second[k][j] for k in range(3)) for j in range(3)] for i in range(3)]
@@ -179,12 +174,17 @@
         tab_ref[pl.ds(f, ROWS, stride=16), :] = world[f] if f < 10 else zeros
 
     nt = (((1,), (1,)), ((), ()))
-    vox_iota = lax.broadcasted_iota(jnp.int32, (VOX, LANES), 0).astype(F32).astype(BF16)
-    vox16 = vox.astype(F32).astype(BF16)
-    sums = jnp.zeros((48, VOX), F32)
+    vox_iota = lax.broadcasted_iota(jnp.int32, (LANES, LANES), 0).astype(F32).astype(BF16)
+    vox16 = jnp.where(vox < 0, -1, vox % LANES).astype(F32).astype(BF16)
+    vhigh = [one_hot(vox < LANES), one_hot(vox >= LANES)]
+    sums = jnp.zeros((96, LANES), F32)
     for t in range(TM):
         hot = jnp.concatenate([hot16(vox_iota, vox16[r : r + 1, :]) for r in range(4 * t, 4 * t + 4)], axis=1)
-        sums = sums + lax.dot_general(split3(wide(tab_ref, t, 16)), hot, nt, preferred_element_type=F32)
+        w = split3(wide(tab_ref, t, 16))
+        masks = [jnp.concatenate([h[r : r + 1, :] for r in range(4 * t, 4 * t + 4)], axis=1) for h in vhigh]
+        left = jnp.concatenate([w * m for m in masks], axis=0)
+        sums = sums + lax.dot_general(left, hot, nt, preferred_element_type=F32)
+    sums = jnp.concatenate([sums[:48], sums[48:]], axis=1)
     sums = fold3(sums)
     count = jnp.maximum(sums[9:10] * PTS, 1.0)
     angles = angles_ref[...]

time: 48.9 us -> 48.5 us (level)
  no operation moved by 1% of the time
where the time goes in v3:
time: 48.5 us; the launch traced here: 48.3 us
  blocking collectives  40.1 us (83%)
  Pallas kernels  7.56 us (16%)
  between operations  0.66 us (1%)
    all_to_all x1, blocking collectives, local(): lax.all_to_all(sent.reshape(devices, 1, SENT_ROWS * LANES), axes, 0, 0, t...  22.9 us
    all_to_all x1, blocking collectives, local(): lax.all_to_all(shares.reshape(devices, 1, BACK_ROWS * LANES), axes, 0, 0,...  17.2 us
    pallas_call x1, Pallas kernels, moments(): pl.pallas_call(moments_kernel, in_specs=[anywhere] * 4, out_shape=jax.Sha...  4.41 us
    pallas_call x1, Pallas kernels, owner(): pl.pallas_call(owner_kernel, out_shape=(jax.ShapeDtypeStruct((devices * B...  2.36 us

profile of v3, /device:TPU:1, one launch (start us, length us, event | category | flops | bytes accessed | tf_op | source)
XLA Modules:
  0.0 48.3 jit_solution(11360134223562158788)
XLA Ops:
  0.6 0.0 copy-start
  0.6 4.4 %shard_map.76 = f32[640,128]{1,0:T(8,128)} custom-call(f32[3,4096,128]{2,1,0:T(8,128)} %points_hbm.1, s32[32,128]{1,0:T(8,128)} %bitcast.12, s32[32,128]{1,0:T(8,128)} %bitcast.13, f32[6,32]{1,0:T(8,128)} %poses_hbm.1), custom_call_target="tpu_custom_call" | custom-call | tf_op jit(solution)/shard_map/pallas_call | solution.py:269
  5.1 22.9 %all_to_all.10 = f32[128,1,640]{2,1,0:T(1,128)S(1)} all-to-all(f32[128,1,640]{2,1,0:T(1,128)} %bitcast.11), channel_id=1, replica_groups=mesh['tm'=8,'map'=16] {'tm','map'}, dimensions={0} | all-to-all | bytes 655360 | tf_op jit(solution)/shard_map/all_to_all | solution.py:307
  27.9 0.0 copy-done
  27.9 2.4 %shard_map.77 = (f32[896,128]{1,0:T(8,128)S(1)}, f32[1,256]{1,0:T(1,128)}) custom-call(f32[640,128]{1,0:T(8,128)S(1)} %bitcast.9, f32[2,256]{1,0:T(2,128)S(1)} %copy-done), custom_call_target="tpu_custom_call" | custom-call | tf_op jit(solution)/shard_map/pallas_call | solution.py:287
  30.3 17.2 %all_to_all.11 = f32[128,1,896]{2,1,0:T(1,128)S(1)} all-to-all(f32[128,1,896]{2,1,0:T(1,128)S(1)} %bitcast.10), channel_id=1, replica_groups=mesh['tm'=8,'map'=16] {'tm','map'}, dimensions={0} | all-to-all | bytes 917504 | tf_op jit(solution)/shard_map/all_to_all | solution.py:310
  47.5 0.8 %shard_map.78 = (f32[32,36]{1,0:T(8,128)}, f32[6,32]{1,0:T(8,128)}) custom-call(f32[896,128]{1,0:T(8,128)S(1)} %bitcast.8), custom_call_target="tpu_custom_call" | custom-call | tf_op jit(solution)/shard_map/pallas_call | solution.py:314
Async XLA Ops:
  0.6 27.3 %copy-start = (f32[2,256]{1,0:T(2,128)S(1)}, f32[2,256]{1,0:T(2,128)}, u32[]{:S(2)}) copy-start(f32[2,256]{1,0:T(2,128)} %angles_ref.1) | copy-start | bytes 6148

commit v4 on v3

--- a/solution.py
+++ b/solution.py
@@ -269,7 +269,8 @@
     return pl.pallas_call(
         moments_kernel,
         in_specs=[anywhere] * 4,
-        out_shape=jax.ShapeDtypeStruct((devices * SENT_ROWS, LANES), F32),
+        out_shape=pltpu.VMEM((devices * SENT_ROWS, LANES), F32),
+        out_specs=pl.BlockSpec(memory_space=pltpu.VMEM),
         scratch_shapes=[
             pltpu.VMEM((9, ROWS, LANES), F32),
             pltpu.VMEM(points.shape, F32),

time: 48.5 us -> 47.5 us (0.979)
  Pallas kernels: 7.56 us -> 6.84 us
    pallas_call x1, Pallas kernels: 4.41 us -> 3.69 us  [moments(): pl.pallas_call(moments_kernel, in_specs=[anywhere] * 4, out_shape=pltpu.V...]
where the time goes in v4:
time: 47.5 us; the launch traced here: 47.4 us
  blocking collectives  39.9 us (84%)
  Pallas kernels  6.84 us (14%)
  between operations  0.66 us (1%)
    all_to_all x1, blocking collectives, local(): lax.all_to_all(sent.reshape(devices, 1, SENT_ROWS * LANES), axes, 0, 0, t...  22.7 us
    all_to_all x1, blocking collectives, local(): lax.all_to_all(shares.reshape(devices, 1, BACK_ROWS * LANES), axes, 0, 0,...  17.2 us
    pallas_call x1, Pallas kernels, moments(): pl.pallas_call(moments_kernel, in_specs=[anywhere] * 4, out_shape=pltpu.V...  3.69 us
    pallas_call x1, Pallas kernels, owner(): pl.pallas_call(owner_kernel, out_shape=(jax.ShapeDtypeStruct((devices * B...  2.36 us

profile of v4, /device:TPU:1, one launch (start us, length us, event | category | flops | bytes accessed | tf_op | source)
XLA Modules:
  0.0 47.4 jit_solution(8538653550868204734)
XLA Ops:
  0.6 0.0 copy-start
  0.6 3.7 %shard_map.76 = f32[640,128]{1,0:T(8,128)S(1)} custom-call(f32[3,4096,128]{2,1,0:T(8,128)} %points_hbm.1, s32[32,128]{1,0:T(8,128)} %bitcast.12, s32[32,128]{1,0:T(8,128)} %bitcast.13, f32[6,32]{1,0:T(8,128)} %poses_hbm.1), custom_call_target="tpu_custom_call" | custom-call | tf_op jit(solution)/shard_map/pallas_call | solution.py:269
  4.3 22.7 %all_to_all.10 = f32[128,1,640]{2,1,0:T(1,128)S(1)} all-to-all(f32[128,1,640]{2,1,0:T(1,128)S(1)} %bitcast.9), channel_id=1, replica_groups=mesh['tm'=8,'map'=16] {'tm','map'}, dimensions={0} | all-to-all | bytes 655360 | tf_op jit(solution)/shard_map/all_to_all | solution.py:308
  27.0 0.0 copy-done
  27.0 2.4 %shard_map.77 = (f32[896,128]{1,0:T(8,128)S(1)}, f32[1,256]{1,0:T(1,128)}) custom-call(f32[640,128]{1,0:T(8,128)S(1)} %bitcast.10, f32[2,256]{1,0:T(2,128)S(1)} %copy-done), custom_call_target="tpu_custom_call" | custom-call | tf_op jit(solution)/shard_map/pallas_call | solution.py:288
  29.4 17.2 %all_to_all.11 = f32[128,1,896]{2,1,0:T(1,128)S(1)} all-to-all(f32[128,1,896]{2,1,0:T(1,128)S(1)} %bitcast.11), channel_id=1, replica_groups=mesh['tm'=8,'map'=16] {'tm','map'}, dimensions={0} | all-to-all | bytes 917504 | tf_op jit(solution)/shard_map/all_to_all | solution.py:311
  46.6 0.8 %shard_map.78 = (f32[32,36]{1,0:T(8,128)}, f32[6,32]{1,0:T(8,128)}) custom-call(f32[896,128]{1,0:T(8,128)S(1)} %bitcast.8), custom_call_target="tpu_custom_call" | custom-call | tf_op jit(solution)/shard_map/pallas_call | solution.py:315
Async XLA Ops:
  0.6 26.4 %copy-start = (f32[2,256]{1,0:T(2,128)S(1)}, f32[2,256]{1,0:T(2,128)}, u32[]{:S(2)}) copy-start(f32[2,256]{1,0:T(2,128)} %angles_ref.1) | copy-start | bytes 6148

commit v5 on v4

--- a/solution.py
+++ b/solution.py
@@ -62,14 +62,14 @@
     ]
     for c in range(chunks):
         fetch(c).start()
-    for copy in small:
-        copy.start()
-
-    @pl.loop(0, chunks)
-    def _(c):
+        if c == 1:
+            for copy in small:
+                copy.start()
+
+    for c in range(chunks):
         fetch(c).wait()
         for cc in range(size // LANES):
-            span = pl.ds(pl.multiple_of(c * size + cc * LANES, LANES), LANES)
+            span = pl.ds(c * size + cc * LANES, LANES)
             x = points_ref[0, span, :].T
             y = points_ref[1, span, :].T
             z = points_ref[2, span, :].T
@@ -130,14 +130,21 @@
     feats = []
     for k in range(SENT_ROWS):
         rows = [recv_ref[pl.ds(h * SENT_ROWS + k, ROWS, stride=GROUPS * SENT_ROWS), :] for h in range(GROUPS)]
-        feats += swap_groups(rows)
+        if k < SENT_ROWS - 1:
+            feats += swap_groups(rows)
+        else:
+            lane = lax.broadcasted_iota(jnp.int32, (ROWS, LANES), 1) // SLOTS
+            last = rows[0]
+            for h in range(1, GROUPS):
+                last = jnp.where(lane == h, pltpu.roll(rows[h], h * SLOTS, 1), last)
+            feats.append(last)
     p1 = feats[0:3]
     pxx, pyy, pzz, pxy, pxz, pyz = feats[3:9]
     vox = feats[9].astype(jnp.int32)
     scan = feats[10].astype(jnp.int32)
     zeros = jnp.zeros((ROWS, LANES), F32)
-    for f in range(8):
-        tab_ref[pl.ds(f, ROWS, stride=8), :] = feats[11 + f] if f < 6 else zeros
+    for f in range(6):
+        tab_ref[pl.ds(f, ROWS, stride=8), :] = feats[11 + f]
 
     def wide(ref, t, n):
         return jnp.concatenate([ref[pl.ds((t * 4 + i) * n, n), :] for i in range(4)], axis=1)
@@ -170,8 +177,8 @@
         m2[i, j] = sum(half[i][k] * rot[j][k] for k in range(3)) + rp[i] * tr[j] + tr[i] * m1[j]
         m2[j, i] = m2[i, j]
     world = m1 + [m2[0, 0], m2[1, 1], m2[2, 2], m2[0, 1], m2[0, 2], m2[1, 2], jnp.ones((ROWS, LANES), F32)]
-    for f in range(16):
-        tab_ref[pl.ds(f, ROWS, stride=16), :] = world[f] if f < 10 else zeros
+    for f in range(10):
+        tab_ref[pl.ds(f, ROWS, stride=16), :] = world[f]
 
     nt = (((1,), (1,)), ((), ()))
     vox_iota = lax.broadcasted_iota(jnp.int32, (LANES, LANES), 0).astype(F32).astype(BF16)
@@ -226,7 +233,8 @@
     features = [terms[i, j] for i in range(6) for j in range(i, 6)] + grad
     for row in range(32):
         f = row % 8 * 4 + row // 8
-        feat_ref[pl.ds(row, ROWS, stride=32), :] = features[f] if f < 27 else zeros
+        if f < 28:
+            feat_ref[pl.ds(row, ROWS, stride=32), :] = features[f] if f < 27 else zeros
 
     high = [one_hot(scan >= 256) if k else one_hot(scan < 256) for k in range(2)]
     low = (scan % 256).astype(F32).T.astype(BF16)
@@ -265,7 +273,7 @@
 
 def moments(points, voxel_ids, scan_ids, poses, devices):
     anywhere = pl.BlockSpec(memory_space=pl.ANY)
-    chunks = 8
+    chunks = 4
     return pl.pallas_call(
         moments_kernel,
         in_specs=[anywhere] * 4,

time: 47.5 us -> 47.4 us (level)
  no operation moved by 1% of the time
where the time goes in v5:
time: 47.4 us; the launch traced here: 47.2 us
  blocking collectives  39.9 us (84%)
  Pallas kernels  6.72 us (14%)
  between operations  0.66 us (1%)
    all_to_all x1, blocking collectives, local(): lax.all_to_all(sent.reshape(devices, 1, SENT_ROWS * LANES), axes, 0, 0, t...  22.7 us
    all_to_all x1, blocking collectives, local(): lax.all_to_all(shares.reshape(devices, 1, BACK_ROWS * LANES), axes, 0, 0,...  17.2 us
    pallas_call x1, Pallas kernels, moments(): pl.pallas_call(moments_kernel, in_specs=[anywhere] * 4, out_shape=pltpu.V...  3.65 us
    pallas_call x1, Pallas kernels, owner(): pl.pallas_call(owner_kernel, out_shape=(jax.ShapeDtypeStruct((devices * B...  2.28 us

profile of v5, /device:TPU:1, one launch (start us, length us, event | category | flops | bytes accessed | tf_op | source)
XLA Modules:
  0.0 47.2 jit_solution(2756854696677637433)
XLA Ops:
  0.6 0.0 copy-start
  0.6 3.6 %shard_map.76 = f32[640,128]{1,0:T(8,128)S(1)} custom-call(f32[3,4096,128]{2,1,0:T(8,128)} %points_hbm.1, s32[32,128]{1,0:T(8,128)} %bitcast.12, s32[32,128]{1,0:T(8,128)} %bitcast.13, f32[6,32]{1,0:T(8,128)} %poses_hbm.1), custom_call_target="tpu_custom_call" | custom-call | tf_op jit(solution)/shard_map/pallas_call | solution.py:277
  4.3 22.7 %all_to_all.10 = f32[128,1,640]{2,1,0:T(1,128)S(1)} all-to-all(f32[128,1,640]{2,1,0:T(1,128)S(1)} %bitcast.9), channel_id=1, replica_groups=mesh['tm'=8,'map'=16] {'tm','map'}, dimensions={0} | all-to-all | bytes 655360 | tf_op jit(solution)/shard_map/all_to_all | solution.py:316
  27.0 0.0 copy-done
  27.0 2.3 %shard_map.77 = (f32[896,128]{1,0:T(8,128)S(1)}, f32[1,256]{1,0:T(1,128)}) custom-call(f32[640,128]{1,0:T(8,128)S(1)} %bitcast.10, f32[2,256]{1,0:T(2,128)S(1)} %copy-done), custom_call_target="tpu_custom_call" | custom-call | tf_op jit(solution)/shard_map/pallas_call | solution.py:296
  29.3 17.2 %all_to_all.11 = f32[128,1,896]{2,1,0:T(1,128)S(1)} all-to-all(f32[128,1,896]{2,1,0:T(1,128)S(1)} %bitcast.11), channel_id=1, replica_groups=mesh['tm'=8,'map'=16] {'tm','map'}, dimensions={0} | all-to-all | bytes 917504 | tf_op jit(solution)/shard_map/all_to_all | solution.py:319
  46.4 0.8 %shard_map.78 = (f32[32,36]{1,0:T(8,128)}, f32[6,32]{1,0:T(8,128)}) custom-call(f32[896,128]{1,0:T(8,128)S(1)} %bitcast.8), custom_call_target="tpu_custom_call" | custom-call | tf_op jit(solution)/shard_map/pallas_call | solution.py:323
Async XLA Ops:
  0.6 26.3 %copy-start = (f32[2,256]{1,0:T(2,128)S(1)}, f32[2,256]{1,0:T(2,128)}, u32[]{:S(2)}) copy-start(f32[2,256]{1,0:T(2,128)} %angles_ref.1) | copy-start | bytes 6148

commit v6 on v5

--- a/solution.py
+++ b/solution.py
@@ -184,13 +184,13 @@
     vox_iota = lax.broadcasted_iota(jnp.int32, (LANES, LANES), 0).astype(F32).astype(BF16)
     vox16 = jnp.where(vox < 0, -1, vox % LANES).astype(F32).astype(BF16)
     vhigh = [one_hot(vox < LANES), one_hot(vox >= LANES)]
-    sums = jnp.zeros((96, LANES), F32)
+    hots, lefts = [], []
     for t in range(TM):
-        hot = jnp.concatenate([hot16(vox_iota, vox16[r : r + 1, :]) for r in range(4 * t, 4 * t + 4)], axis=1)
+        hots += [hot16(vox_iota, vox16[r : r + 1, :]) for r in range(4 * t, 4 * t + 4)]
         w = split3(wide(tab_ref, t, 16))
         masks = [jnp.concatenate([h[r : r + 1, :] for r in range(4 * t, 4 * t + 4)], axis=1) for h in vhigh]
-        left = jnp.concatenate([w * m for m in masks], axis=0)
-        sums = sums + lax.dot_general(left, hot, nt, preferred_element_type=F32)
+        lefts.append(jnp.concatenate([w * m for m in masks], axis=0))
+    sums = lax.dot_general(jnp.concatenate(lefts, axis=1), jnp.concatenate(hots, axis=1), nt, preferred_element_type=F32)
     sums = jnp.concatenate([sums[:48], sums[48:]], axis=1)
     sums = fold3(sums)
     count = jnp.maximum(sums[9:10] * PTS, 1.0)

time: 47.4 us -> 47.4 us (level)
  no operation moved by 1% of the time
where the time goes in v6:
time: 47.4 us; the launch traced here: 47.2 us
  blocking collectives  39.9 us (84%)
  Pallas kernels  6.72 us (14%)
  between operations  0.66 us (1%)
    all_to_all x1, blocking collectives, local(): lax.all_to_all(sent.reshape(devices, 1, SENT_ROWS * LANES), axes, 0, 0, t...  22.7 us
    all_to_all x1, blocking collectives, local(): lax.all_to_all(shares.reshape(devices, 1, BACK_ROWS * LANES), axes, 0, 0,...  17.2 us
    pallas_call x1, Pallas kernels, moments(): pl.pallas_call(moments_kernel, in_specs=[anywhere] * 4, out_shape=pltpu.V...  3.65 us
    pallas_call x1, Pallas kernels, owner(): pl.pallas_call(owner_kernel, out_shape=(jax.ShapeDtypeStruct((devices * B...  2.28 us

profile of v6, /device:TPU:1, one launch (start us, length us, event | category | flops | bytes accessed | tf_op | source)
XLA Modules:
  0.0 47.2 jit_solution(6182255070936056707)
XLA Ops:
  0.6 0.0 copy-start
  0.6 3.6 %shard_map.76 = f32[640,128]{1,0:T(8,128)S(1)} custom-call(f32[3,4096,128]{2,1,0:T(8,128)} %points_hbm.1, s32[32,128]{1,0:T(8,128)} %bitcast.12, s32[32,128]{1,0:T(8,128)} %bitcast.13, f32[6,32]{1,0:T(8,128)} %poses_hbm.1), custom_call_target="tpu_custom_call" | custom-call | tf_op jit(solution)/shard_map/pallas_call | solution.py:277
  4.3 22.7 %all_to_all.10 = f32[128,1,640]{2,1,0:T(1,128)S(1)} all-to-all(f32[128,1,640]{2,1,0:T(1,128)S(1)} %bitcast.9), channel_id=1, replica_groups=mesh['tm'=8,'map'=16] {'tm','map'}, dimensions={0} | all-to-all | bytes 655360 | tf_op jit(solution)/shard_map/all_to_all | solution.py:316
  27.0 0.0 copy-done
  27.0 2.3 %shard_map.77 = (f32[896,128]{1,0:T(8,128)S(1)}, f32[1,256]{1,0:T(1,128)}) custom-call(f32[640,128]{1,0:T(8,128)S(1)} %bitcast.10, f32[2,256]{1,0:T(2,128)S(1)} %copy-done), custom_call_target="tpu_custom_call" | custom-call | tf_op jit(solution)/shard_map/pallas_call | solution.py:296
  29.3 17.2 %all_to_all.11 = f32[128,1,896]{2,1,0:T(1,128)S(1)} all-to-all(f32[128,1,896]{2,1,0:T(1,128)S(1)} %bitcast.11), channel_id=1, replica_groups=mesh['tm'=8,'map'=16] {'tm','map'}, dimensions={0} | all-to-all | bytes 917504 | tf_op jit(solution)/shard_map/all_to_all | solution.py:319
  46.4 0.8 %shard_map.78 = (f32[32,36]{1,0:T(8,128)}, f32[6,32]{1,0:T(8,128)}) custom-call(f32[896,128]{1,0:T(8,128)S(1)} %bitcast.8), custom_call_target="tpu_custom_call" | custom-call | tf_op jit(solution)/shard_map/pallas_call | solution.py:323
Async XLA Ops:
  0.6 26.3 %copy-start = (f32[2,256]{1,0:T(2,128)S(1)}, f32[2,256]{1,0:T(2,128)}, u32[]{:S(2)}) copy-start(f32[2,256]{1,0:T(2,128)} %angles_ref.1) | copy-start | bytes 6148
